TPU v7x, 32 devices: a whole 2x2x4 slice. The times are simulated.
32 devices in a mesh: chan: 8 (over y, x, core), tm: 4 (over z).
Axes of the slice: x: 2, y: 2, z: 4, core: 2. Of those that a mesh axis runs over, the one named last changes fastest.
Arguments:
- raw_strain: float32 [512, 4096], P('chan', 'tm'), may hold values from -2000 to 2000
- fir_taps: float32 [64], replicated, may hold values from -0.75 to 0.75
- block_mask: int32 [8, 8], replicated, may hold values 0 or 1
Outputs:
- correlations: float32 [128, 512, 512], P('tm', 'chan')
All inputs are finite; a program needn't handle non-finite values.
Results may differ from a plain program's by a relative error of at most 0.0054.
Values may be sent and summed in bfloat16 or wider, within the bound.
A program may use at most 64 MiB of HBM per device.

v0:
```python
import functools
import math

import jax
import jax.numpy as jnp
from jax import lax
from jax.experimental import pallas as pl
from jax.experimental.pallas import tpu as pltpu
from jax.sharding import PartitionSpec as P

DECIM = 8
TAPS = 64
LAGS = 128
LANES = 128
WIDE = 2 * LANES
MESH = pl.DeviceIdType.MESH


def filter_tile(taps_ref):
    row = lax.broadcasted_iota(jnp.int32, (DECIM, LANES), 0)
    lane = lax.broadcasted_iota(jnp.int32, (DECIM, LANES), 1)
    which = DECIM * lane + (DECIM - 1) - row
    base = jnp.zeros((DECIM, LANES), jnp.float32)
    for tap in range(TAPS):
        base = jnp.where(which == tap, taps_ref[tap], base)
    rows = [base if m == 0 else pltpu.roll(base, m, 1) for m in range(WIDE // DECIM)]
    return jnp.concatenate(rows, axis=0)


def flipped(index, bits):
    place = 1
    while place <= bits:
        if bits & place:
            index = index + place - 2 * place * lax.rem(index // place, 2)
        place *= 2
    return index


def whiten(pieces, samples):
    squares = pieces[0] * pieces[0]
    for piece in pieces[1:]:
        squares = squares + piece * piece
    root = jnp.sqrt(jnp.sum(squares, axis=1, keepdims=True) * (1.0 / samples) + 1e-06)
    return [(piece / root).astype(jnp.bfloat16) for piece in pieces]


def gather_kernel(
    chans, tms, taps_hbm, raw_hbm, mask_hbm, left, right, weight_ref,
    raw_v, taps_ref, mask_ref, halo, record,
    load_sems, halo_send, halo_recv, z_send, z_recv, c_send, c_recv, s_send, s_recv,
):
    rows, span = raw_v.shape
    outputs = span // DECIM
    samples = outputs * tms
    chips = chans // 2
    lag_count = left.shape[0] // rows
    c = lax.axis_index("chan")
    z = lax.axis_index("tm")
    chip, core = c // 2, lax.rem(c, 2)
    sibling = 2 * chip + (1 - core)

    load_raw = pltpu.make_async_copy(raw_hbm, raw_v, load_sems.at[0])
    load_taps = pltpu.make_async_copy(taps_hbm, taps_ref, load_sems.at[1])
    load_mask = pltpu.make_async_copy(mask_hbm, mask_ref, load_sems.at[2])
    load_taps.start()
    load_raw.start()
    load_mask.start()

    z_peers = [
        flipped(z, d) if tms & (tms - 1) == 0 else lax.rem(z + d, tms) for d in range(1, tms)
    ]
    z_sources = [
        flipped(z, d) if tms & (tms - 1) == 0 else lax.rem(z - d + tms, tms)
        for d in range(1, tms)
    ]
    power = chips & (chips - 1) == 0
    c_peers = [
        2 * (flipped(chip, d) if power else lax.rem(chip + d, chips)) + core
        for d in range(1, chips)
    ]
    c_sources = [
        2 * (flipped(chip, d) if power else lax.rem(chip - d + chips, chips)) + core
        for d in range(1, chips)
    ]
    barrier = pltpu.get_barrier_semaphore()
    for peer in z_peers:
        pl.semaphore_signal(barrier, inc=1, device_id=(c, peer), device_id_type=MESH)
    for peer in c_peers + [sibling]:
        pl.semaphore_signal(barrier, inc=1, device_id=(peer, z), device_id_type=MESH)

    load_taps.wait()
    table = filter_tile(taps_ref)
    load_raw.wait()
    pl.semaphore_wait(barrier, tms - 1 + chips)

    halo_copy = pltpu.make_async_remote_copy(
        src_ref=raw_v.at[:, pl.ds(span - LANES, LANES)],
        dst_ref=halo,
        send_sem=halo_send,
        recv_sem=halo_recv,
        device_id=(c, jnp.minimum(z + 1, tms - 1)),
        device_id_type=MESH,
    )

    @pl.when(z < tms - 1)
    def _():
        halo_copy.start()

    @pl.when(z == 0)
    def _():
        halo[...] = jnp.zeros_like(halo)

    parts = span // WIDE
    stacked = jnp.concatenate([raw_v[:, q * WIDE : (q + 1) * WIDE] for q in range(parts)], axis=0)
    product = jnp.dot(
        stacked, table, precision=lax.Precision.HIGHEST, preferred_element_type=jnp.float32
    )
    step = WIDE // DECIM
    lane = lax.broadcasted_iota(jnp.int32, (rows, LANES), 1)
    total = product[:rows]
    for q in range(1, parts):
        turned = pltpu.roll(product[q * rows : (q + 1) * rows], q * step, 1)
        if q == parts - 1:
            turned = jnp.where(lane < DECIM, 0.0, turned)
        total = total + turned

    load_mask.wait()
    channels = rows * chans
    column = lax.broadcasted_iota(jnp.int32, weight_ref.shape, 1) // rows
    weight = jnp.zeros(weight_ref.shape, jnp.float32)
    for b in range(chans):
        weight = jnp.where(column == b, mask_ref[c, b].astype(jnp.float32), weight)
    weight_ref[...] = weight * (1.0 / math.sqrt(samples))

    @pl.when(z > 0)
    def _():
        halo_copy.wait_recv()

    before = jnp.dot(
        halo[...], table[WIDE - LANES :], precision=lax.Precision.HIGHEST,
        preferred_element_type=jnp.float32,
    )
    before = pltpu.roll(before, LANES - step, 1)
    total = total + jnp.where(lane < DECIM, before, 0.0)

    def rows_of(owner):
        return pl.ds(pl.multiple_of(owner * rows, rows), rows)

    record[z, rows_of(c)] = total.astype(jnp.bfloat16)

    def push(when, owner, target, send, recv):
        piece = record.at[when, rows_of(owner)]
        return pltpu.make_async_remote_copy(
            src_ref=piece, dst_ref=piece, send_sem=send, recv_sem=recv,
            device_id=target, device_id_type=MESH,
        )

    sent = []

    def start(copy):
        copy.start()
        sent.append(copy)

    def spread(when, slot):
        for d in range(1, chips):
            start(push(when, c, (c_peers[d - 1], z), c_send.at[d - 1, slot], c_recv.at[d - 1, slot]))
        start(push(when, c, (sibling, z), s_send.at[0, slot], s_recv.at[0, slot]))

    def relay(d, slot):
        when = z if slot == 0 else z_sources[slot - 1]
        owner = c_sources[d - 1]
        push(when, owner, (owner, z), c_send.at[d - 1, slot], c_recv.at[d - 1, slot]).wait_recv()
        start(push(when, owner, (sibling, z), s_send.at[d, slot], s_recv.at[d, slot]))

    for d in range(1, tms):
        start(push(z, c, (c, z_peers[d - 1]), z_send.at[d - 1], z_recv.at[d - 1]))
    spread(z, 0)
    for d in range(1, tms):
        source = z_sources[d - 1]
        push(source, c, (c, source), z_send.at[d - 1], z_recv.at[d - 1]).wait_recv()
        spread(source, d)
    for d in range(1, chips):
        relay(d, 0)

    def whiten_rows(owner):
        pieces = [record[k, rows_of(owner)].astype(jnp.float32) for k in range(tms)]
        whites = whiten(pieces, samples)
        for k, white in enumerate(whites):
            right[rows_of(owner), k * outputs : (k + 1) * outputs] = white
        return whites

    tiles = [white.astype(jnp.float32) for white in whiten_rows(c)]
    group = min(4, lag_count)

    def some_lags(turn, carry):
        for inner in range(group):
            number = turn * group + inner
            lag = z * lag_count + number
            earlier = jnp.zeros((rows, LANES), jnp.float32)
            for k, tile in enumerate(tiles):
                turned = pltpu.roll(tile, lag, 1)
                left[rows_of(number), k * LANES : (k + 1) * LANES] = jnp.where(
                    lane < lag, earlier, turned
                ).astype(jnp.bfloat16)
                earlier = turned
        return carry

    lax.fori_loop(0, lag_count // group, some_lags, 0)

    for slot in range(1, tms):
        for d in range(1, chips):
            relay(d, slot)
    for d in range(1, chips):
        whiten_rows(c_sources[d - 1])
    for d in range(chips):
        owner = sibling if d == 0 else c_sources[d - 1] + 1 - 2 * core
        for slot in range(tms):
            when = z if slot == 0 else z_sources[slot - 1]
            push(when, owner, (sibling, z), s_send.at[d, slot], s_recv.at[d, slot]).wait_recv()
        whiten_rows(owner)

    @pl.when(z < tms - 1)
    def _():
        halo_copy.wait_send()

    for copy in sent:
        copy.wait_send()


def correlate_kernel(left, right, weight_ref, out_hbm, out_v, sems):
    channels, samples = right.shape
    lag_count, rows = out_v.shape[:2]
    chunks = sems.shape[0]
    per = lag_count // chunks
    wide = min(channels, 512)
    copies = []
    for chunk in range(chunks):
        lags = pl.ds(chunk * per, per)

        def one(part, carry):
            at = pl.ds(pl.multiple_of(part * wide, wide), wide)
            product = lax.dot_general(
                left[chunk * per * rows : (chunk + 1) * per * rows], right[at],
                (((1,), (1,)), ((), ())), preferred_element_type=jnp.float32,
            )
            out_v[lags, :, at] = (product * weight_ref[0:1, at]).reshape(per, rows, wide)
            return carry

        if channels == wide:
            one(0, 0)
        else:
            lax.fori_loop(0, channels // wide, one, 0)
        copy = pltpu.make_async_copy(out_v.at[lags], out_hbm.at[lags], sems.at[chunk])
        copy.start()
        copies.append(copy)
    for copy in copies:
        copy.wait()


def per_device(raw_strain, fir_taps, block_mask, *, chans, tms):
    rows, span = raw_strain.shape
    outputs = span // DECIM
    samples = outputs * tms
    channels = rows * chans
    chips = chans // 2
    lag_count = LAGS // tms
    hbm = pl.BlockSpec(memory_space=pltpu.HBM)
    vmem = pl.BlockSpec(memory_space=pltpu.VMEM)
    dma = pltpu.SemaphoreType.DMA
    left, right, weight = pl.pallas_call(
        functools.partial(gather_kernel, chans, tms),
        out_shape=[
            jax.ShapeDtypeStruct((lag_count * rows, samples), jnp.bfloat16),
            jax.ShapeDtypeStruct((channels, samples), jnp.bfloat16),
            jax.ShapeDtypeStruct((8, channels), jnp.float32),
        ],
        in_specs=[hbm] * 3,
        out_specs=[vmem] * 3,
        scratch_shapes=[
            pltpu.VMEM((rows, span), jnp.float32),
            pltpu.SMEM((TAPS,), jnp.float32),
            pltpu.SMEM((chans, chans), jnp.int32),
            pltpu.VMEM((rows, LANES), jnp.float32),
            pltpu.VMEM((tms, channels, outputs), jnp.bfloat16),
            dma((3,)),
            dma,
            dma,
            dma((tms - 1,)),
            dma((tms - 1,)),
            dma((chips - 1, tms)),
            dma((chips - 1, tms)),
            dma((chips, tms)),
            dma((chips, tms)),
        ],
        compiler_params=pltpu.CompilerParams(
            collective_id=0, has_side_effects=True, vmem_limit_bytes=32 * 2**20
        ),
        name="gather",
    )(*[pltpu.with_memory_space_constraint(a, pltpu.HBM) for a in (fir_taps, raw_strain, block_mask)])

    chunks = min(8, lag_count)
    return pl.pallas_call(
        correlate_kernel,
        out_shape=jax.ShapeDtypeStruct((lag_count, rows, channels), jnp.float32),
        in_specs=[vmem] * 3,
        out_specs=hbm,
        scratch_shapes=[pltpu.VMEM((lag_count, rows, channels), jnp.float32), dma((chunks,))],
        compiler_params=pltpu.CompilerParams(vmem_limit_bytes=32 * 2**20),
        name="correlate",
    )(left, right, weight)


def solution(mesh):
    placed = (P("chan", "tm"), P(), P())
    return jax.shard_map(
        functools.partial(per_device, chans=mesh.shape["chan"], tms=mesh.shape["tm"]),
        mesh=mesh, in_specs=placed, out_specs=P("tm", "chan", None), check_vma=False,
    )
```

profile of v0, /device:TPU:0, one launch (start us, length us, event | category | flops | bytes accessed | tf_op | source)
XLA Modules:
  0.0 20.1 jit_solution(12927570110677444985)
XLA Ops:
  0.0 17.6 %gather.1 = (bf16[2048,512]{1,0:T(8,128)(2,1)S(1)}, bf16[512,512]{1,0:T(8,128)(2,1)S(1)}, f32[8,512]{1,0:T(8,128)S(1)}) custom-call(f32[64]{0:T(128)} %taps_hbm.1, f32[64,1024]{1,0:T(8,128)} %raw_hbm.1, s32[8,8]{1,0:T(8,128)} %mask_hbm.1), custom_call_target="tpu_custom_call" | custom-call | tf_op jit(solution)/shard_map/gather/pallas_call | solution.py:270
  17.6 2.4 %correlate.1 = f32[32,64,512]{2,1,0:T(8,128)} custom-call(bf16[2048,512]{1,0:T(8,128)(2,1)S(1)} %get-tuple-element.8.left, bf16[512,512]{1,0:T(8,128)(2,1)S(1)} %get-tuple-element.9.right, f32[8,512]{1,0:T(8,128)S(1)} %get-tuple-element.10.weight_ref), custom_call_target="tpu_custom_call" | custom-call | tf_op jit(solution)/shard_map/correlate/pallas_call | solution.py:302
where the time goes:
time: 20.3 us; the launch traced here: 20.1 us
  Pallas kernels  20 us (99%)
    pallas_call x1, Pallas kernels, per_device(): pl.pallas_call(functools.partial(gather_kernel, chans, tms), out_shape=[j...  17.6 us
    pallas_call x1, Pallas kernels, per_device(): pl.pallas_call(correlate_kernel, out_shape=jax.ShapeDtypeStruct((lag_coun...  2.4 us

commit v1 on v0

--- a/solution.py
+++ b/solution.py
@@ -12,6 +12,7 @@
 TAPS = 64
 LAGS = 128
 LANES = 128
+CUTS = 1
 WIDE = 2 * LANES
 MESH = pl.DeviceIdType.MESH
 
@@ -46,8 +47,8 @@
 
 def gather_kernel(
     chans, tms, taps_hbm, raw_hbm, mask_hbm, left, right, weight_ref,
-    raw_v, taps_ref, mask_ref, halo, record,
-    load_sems, halo_send, halo_recv, z_send, z_recv, c_send, c_recv, s_send, s_recv,
+    raw_v, taps_ref, mask_ref, ends, record,
+    load_sems, e_send, e_recv, z_send, z_recv, c_send, c_recv, s_send, s_recv,
 ):
     rows, span = raw_v.shape
     outputs = span // DECIM
@@ -91,24 +92,6 @@
     load_taps.wait()
     table = filter_tile(taps_ref)
     load_raw.wait()
-    pl.semaphore_wait(barrier, tms - 1 + chips)
-
-    halo_copy = pltpu.make_async_remote_copy(
-        src_ref=raw_v.at[:, pl.ds(span - LANES, LANES)],
-        dst_ref=halo,
-        send_sem=halo_send,
-        recv_sem=halo_recv,
-        device_id=(c, jnp.minimum(z + 1, tms - 1)),
-        device_id_type=MESH,
-    )
-
-    @pl.when(z < tms - 1)
-    def _():
-        halo_copy.start()
-
-    @pl.when(z == 0)
-    def _():
-        halo[...] = jnp.zeros_like(halo)
 
     parts = span // WIDE
     stacked = jnp.concatenate([raw_v[:, q * WIDE : (q + 1) * WIDE] for q in range(parts)], axis=0)
@@ -121,9 +104,43 @@
     for q in range(1, parts):
         turned = pltpu.roll(product[q * rows : (q + 1) * rows], q * step, 1)
         if q == parts - 1:
+            past = jnp.where(lane < DECIM, turned, 0.0)
             turned = jnp.where(lane < DECIM, 0.0, turned)
         total = total + turned
 
+    record[z] = total.astype(jnp.bfloat16)
+    both = jnp.where(lane < DECIM, total, jnp.where(lane < 2 * DECIM, pltpu.roll(past, DECIM, 1), 0.0))
+    square = jnp.concatenate([both, jnp.zeros((LANES - rows, LANES), jnp.float32)], axis=0)
+    ends[z] = square.T[: 2 * DECIM]
+
+    def rows_of(owner):
+        return pl.ds(pl.multiple_of(owner * rows, rows), rows)
+
+    def share(ref, when, target, send, recv):
+        return pltpu.make_async_remote_copy(
+            src_ref=ref.at[when], dst_ref=ref.at[when], send_sem=send, recv_sem=recv,
+            device_id=(c, target), device_id_type=MESH,
+        )
+
+    cut = rows // CUTS
+
+    def push(owner, part, target, send, recv):
+        piece = right.at[pl.ds(pl.multiple_of(owner * rows + part * cut, cut), cut)]
+        return pltpu.make_async_remote_copy(
+            src_ref=piece, dst_ref=piece, send_sem=send, recv_sem=recv,
+            device_id=(target, z), device_id_type=MESH,
+        )
+
+    sent = []
+
+    def start(copy):
+        copy.start()
+        sent.append(copy)
+
+    pl.semaphore_wait(barrier, tms - 1 + chips)
+    for d in reversed(range(1, tms)):
+        start(share(ends, z, z_peers[d - 1], e_send.at[d - 1], e_recv.at[d - 1]))
+        start(share(record, z, z_peers[d - 1], z_send.at[d - 1], z_recv.at[d - 1]))
     load_mask.wait()
     channels = rows * chans
     column = lax.broadcasted_iota(jnp.int32, weight_ref.shape, 1) // rows
@@ -132,64 +149,42 @@
         weight = jnp.where(column == b, mask_ref[c, b].astype(jnp.float32), weight)
     weight_ref[...] = weight * (1.0 / math.sqrt(samples))
 
-    @pl.when(z > 0)
-    def _():
-        halo_copy.wait_recv()
-
-    before = jnp.dot(
-        halo[...], table[WIDE - LANES :], precision=lax.Precision.HIGHEST,
-        preferred_element_type=jnp.float32,
-    )
-    before = pltpu.roll(before, LANES - step, 1)
-    total = total + jnp.where(lane < DECIM, before, 0.0)
-
-    def rows_of(owner):
-        return pl.ds(pl.multiple_of(owner * rows, rows), rows)
-
-    record[z, rows_of(c)] = total.astype(jnp.bfloat16)
-
-    def push(when, owner, target, send, recv):
-        piece = record.at[when, rows_of(owner)]
-        return pltpu.make_async_remote_copy(
-            src_ref=piece, dst_ref=piece, send_sem=send, recv_sem=recv,
-            device_id=target, device_id_type=MESH,
-        )
-
-    sent = []
-
-    def start(copy):
-        copy.start()
-        sent.append(copy)
-
-    def spread(when, slot):
-        for d in range(1, chips):
-            start(push(when, c, (c_peers[d - 1], z), c_send.at[d - 1, slot], c_recv.at[d - 1, slot]))
-        start(push(when, c, (sibling, z), s_send.at[0, slot], s_recv.at[0, slot]))
-
-    def relay(d, slot):
-        when = z if slot == 0 else z_sources[slot - 1]
-        owner = c_sources[d - 1]
-        push(when, owner, (owner, z), c_send.at[d - 1, slot], c_recv.at[d - 1, slot]).wait_recv()
-        start(push(when, owner, (sibling, z), s_send.at[d, slot], s_recv.at[d, slot]))
-
-    for d in range(1, tms):
-        start(push(z, c, (c, z_peers[d - 1]), z_send.at[d - 1], z_recv.at[d - 1]))
-    spread(z, 0)
     for d in range(1, tms):
         source = z_sources[d - 1]
-        push(source, c, (c, source), z_send.at[d - 1], z_recv.at[d - 1]).wait_recv()
-        spread(source, d)
-    for d in range(1, chips):
-        relay(d, 0)
-
-    def whiten_rows(owner):
-        pieces = [record[k, rows_of(owner)].astype(jnp.float32) for k in range(tms)]
-        whites = whiten(pieces, samples)
-        for k, white in enumerate(whites):
-            right[rows_of(owner), k * outputs : (k + 1) * outputs] = white
-        return whites
-
-    tiles = [white.astype(jnp.float32) for white in whiten_rows(c)]
+        share(ends, source, source, e_send.at[d - 1], e_recv.at[d - 1]).wait_recv()
+        share(record, source, source, z_send.at[d - 1], z_recv.at[d - 1]).wait_recv()
+
+    held = LANES // (2 * DECIM)
+    turned_ends = []
+    for base in range(0, tms, held):
+        few = [ends[k] for k in range(base, min(base + held, tms))]
+        short = LANES - 2 * DECIM * len(few)
+        if short:
+            few.append(jnp.zeros((short, LANES), jnp.float32))
+        turned_ends.append(jnp.concatenate(few, axis=0).T[:rows])
+
+    def end_of(k, tail):
+        at = 2 * DECIM * (k % held) + DECIM * tail
+        return pltpu.roll(turned_ends[k // held], (LANES - at) % LANES, 1)
+
+    pieces = []
+    for k in range(tms):
+        edge = end_of(k, 0)
+        if k:
+            edge = edge + end_of(k - 1, 1)
+        edge = edge.astype(jnp.bfloat16).astype(jnp.float32)
+        pieces.append(jnp.where(lane < DECIM, edge, record[k].astype(jnp.float32)))
+    whites = whiten(pieces, samples)
+    for k, white in enumerate(whites):
+        right[rows_of(c), k * outputs : (k + 1) * outputs] = white
+
+    for part in range(CUTS):
+        start(push(c, part, sibling, s_send.at[0, part], s_recv.at[0, part]))
+    for part in range(CUTS):
+        for d in reversed(range(1, chips)):
+            start(push(c, part, c_peers[d - 1], c_send.at[d - 1, part], c_recv.at[d - 1, part]))
+
+    tiles = [white.astype(jnp.float32) for white in whites]
     group = min(4, lag_count)
 
     def some_lags(turn, carry):
@@ -207,21 +202,15 @@
 
     lax.fori_loop(0, lag_count // group, some_lags, 0)
 
-    for slot in range(1, tms):
+    for part in range(CUTS):
         for d in range(1, chips):
-            relay(d, slot)
-    for d in range(1, chips):
-        whiten_rows(c_sources[d - 1])
-    for d in range(chips):
-        owner = sibling if d == 0 else c_sources[d - 1] + 1 - 2 * core
-        for slot in range(tms):
-            when = z if slot == 0 else z_sources[slot - 1]
-            push(when, owner, (sibling, z), s_send.at[d, slot], s_recv.at[d, slot]).wait_recv()
-        whiten_rows(owner)
-
-    @pl.when(z < tms - 1)
-    def _():
-        halo_copy.wait_send()
+            owner = c_sources[d - 1]
+            push(owner, part, owner, c_send.at[d - 1, part], c_recv.at[d - 1, part]).wait_recv()
+            start(push(owner, part, sibling, s_send.at[d, part], s_recv.at[d, part]))
+    for part in range(CUTS):
+        for d in range(chips):
+            owner = sibling if d == 0 else c_sources[d - 1] + 1 - 2 * core
+            push(owner, part, sibling, s_send.at[d, part], s_recv.at[d, part]).wait_recv()
 
     for copy in sent:
         copy.wait_send()
@@ -280,17 +269,17 @@
             pltpu.VMEM((rows, span), jnp.float32),
             pltpu.SMEM((TAPS,), jnp.float32),
             pltpu.SMEM((chans, chans), jnp.int32),
-            pltpu.VMEM((rows, LANES), jnp.float32),
-            pltpu.VMEM((tms, channels, outputs), jnp.bfloat16),
+            pltpu.VMEM((tms, 2 * DECIM, LANES), jnp.float32),
+            pltpu.VMEM((tms, rows, outputs), jnp.bfloat16),
             dma((3,)),
-            dma,
-            dma,
             dma((tms - 1,)),
             dma((tms - 1,)),
-            dma((chips - 1, tms)),
-            dma((chips - 1, tms)),
-            dma((chips, tms)),
-            dma((chips, tms)),
+            dma((tms - 1,)),
+            dma((tms - 1,)),
+            dma((chips - 1, CUTS)),
+            dma((chips - 1, CUTS)),
+            dma((chips, CUTS)),
+            dma((chips, CUTS)),
         ],
         compiler_params=pltpu.CompilerParams(
             collective_id=0, has_side_effects=True, vmem_limit_bytes=32 * 2**20

time: 20.3 us -> 17.4 us (0.86)
  Pallas kernels: 20 us -> 17.3 us
    pallas_call x1, Pallas kernels: 17.6 us -> 14.9 us  [per_device(): pl.pallas_call(functools.partial(gather_kernel, chans, tms), out_shape=[j...]
where the time goes in v1:
time: 17.4 us; the launch traced here: 17.3 us
  Pallas kernels  17.3 us (99%)
    pallas_call x1, Pallas kernels, per_device(): pl.pallas_call(functools.partial(gather_kernel, chans, tms), out_shape=[j...  14.9 us
    pallas_call x1, Pallas kernels, per_device(): pl.pallas_call(correlate_kernel, out_shape=jax.ShapeDtypeStruct((lag_coun...  2.4 us

profile of v1, /device:TPU:0, one launch (start us, length us, event | category | flops | bytes accessed | tf_op | source)
XLA Modules:
  0.0 17.3 jit_solution(16589825689076142091)
XLA Ops:
  0.0 14.9 %gather.1 = (bf16[2048,512]{1,0:T(8,128)(2,1)S(1)}, bf16[512,512]{1,0:T(8,128)(2,1)S(1)}, f32[8,512]{1,0:T(8,128)S(1)}) custom-call(f32[64]{0:T(128)} %taps_hbm.1, f32[64,1024]{1,0:T(8,128)} %raw_hbm.1, s32[8,8]{1,0:T(8,128)} %mask_hbm.1), custom_call_target="tpu_custom_call" | custom-call | tf_op jit(solution)/shard_map/gather/pallas_call | solution.py:259
  14.9 2.4 %correlate.1 = f32[32,64,512]{2,1,0:T(8,128)} custom-call(bf16[2048,512]{1,0:T(8,128)(2,1)S(1)} %get-tuple-element.8.left, bf16[512,512]{1,0:T(8,128)(2,1)S(1)} %get-tuple-element.9.right, f32[8,512]{1,0:T(8,128)S(1)} %get-tuple-element.10.weight_ref), custom_call_target="tpu_custom_call" | custom-call | tf_op jit(solution)/shard_map/correlate/pallas_call | solution.py:291
